TPU v7x, 512 devices: a whole 4x8x8 slice. The times are simulated.
512 devices in a mesh: row: 8 (over z), col: 16 (over y_hi, x, core), kpart: 4 (over y_lo).
Axes of the slice: x: 4, y: 8 (y_hi: 2, y_lo: 4; y = y_hi * 4 + y_lo), z: 8, core: 2. Of those that a mesh axis runs over, the one named last changes fastest.
Arguments:
- left_cyclic: float32 [2048, 8192], P(('kpart', 'col'), 'row'), may hold values from -6 to 6
- right_cyclic: float32 [2048, 16384], P(('kpart', 'row'), 'col'), may hold values from -0.125 to 0.125
Outputs:
- product: float32 [8192, 16384], P(('row', 'kpart'), 'col')
All inputs are finite; a program needn't handle non-finite values.
Results may differ from a plain program's by a relative error of at most 0.00007.
Values sent between devices are 32-bit elements; how exact they have to be, the bound alone decides.
No kernel may reach another device: no remote copies, remote signals or barrier semaphores. Data moves between devices by JAX's collectives and lax.ppermute only.
A program may use at most 64 MiB of HBM per device.

v0:
```python
import jax
import jax.numpy as jnp
from jax import lax
from jax.sharding import PartitionSpec as P

NB = 64


def contract(left_part, right_part):
    return lax.dot_general(
        left_part,
        right_part,
        (((0,), (0,)), ((), ())),
        precision=lax.Precision.HIGHEST,
        preferred_element_type=jnp.float32,
    )


def shards(left_cyclic, right_cyclic):
    row_count = lax.axis_size("row")
    column_count = lax.axis_size("col")
    slab_left, local_rows = left_cyclic.shape
    group_left = local_rows // (NB * row_count)
    shaped_left = left_cyclic.reshape(slab_left, row_count, group_left, 1, NB)
    moved_left = lax.all_to_all(shaped_left, "row", split_axis=1, concat_axis=3, tiled=True)
    band_left = moved_left.reshape(slab_left, local_rows)
    left_band = lax.all_gather(band_left, "col", axis=0, tiled=True)
    slab_right, local_cols = right_cyclic.shape
    group_right = local_cols // (NB * column_count)
    shaped_right = right_cyclic.reshape(slab_right, column_count, group_right, 1, NB)
    moved_right = lax.all_to_all(shaped_right, "col", split_axis=1, concat_axis=3, tiled=True)
    band_right = moved_right.reshape(slab_right, local_cols)
    right_band = lax.all_gather(band_right, "row", axis=0, tiled=True)
    return lax.psum_scatter(
        contract(left_band, right_band), "kpart", scatter_dimension=0, tiled=True
    )


def solution(mesh):
    placed = (P(("kpart", "col"), "row"), P(("kpart", "row"), "col"))
    return jax.shard_map(
        shards, mesh=mesh, in_specs=placed, out_specs=P(("row", "kpart"), "col"), check_vma=False
    )
```

profile of v0, /device:TPU:57, one launch (start us, length us, event | category | flops | bytes accessed | tf_op | source)
XLA Modules:
  0.0 246.7 jit_solution(4141008044242358849)
XLA Ops:
  6.5 1.1 reshape.19
  7.6 0.2 copy.11
  7.8 0.3 reshape.23
  8.2 16.5 %all_to_all.24 = f32[16,1,4096]{2,1,0:T(1,128)S(1)} all-to-all(f32[16,1,4096]{2,1,0:T(1,128)S(1)} %reshape.23), channel_id=1, replica_groups=mesh['row'=8,'col'=16,'kpart'=4] {'col'}, dimensions={0} | all-to-all | bytes 524288 | tf_op jit(solution)/shard_map/all_to_all | solution.py:31
  24.7 0.5 broadcast
  25.2 1.2 reduce.1
  26.5 0.2 reshape.24
  26.7 0.3 copy.8
  27.0 0.9 reshape.20
  27.9 0.0 all-gather.5.cloned.1.call-update
  27.9 0.0 all-gather.3.cloned.1.call-start
  28.0 0.2 reshape.17
  28.2 0.1 copy.12
  28.3 0.3 reshape.21
  28.5 17.6 %all_to_all.25 = f32[8,1,4096]{2,1,0:T(1,128)S(1)} all-to-all(f32[8,1,4096]{2,1,0:T(1,128)S(1)} %reshape.21), channel_id=1, replica_groups=mesh['row'=8,'col'=16,'kpart'=4] {'row'}, dimensions={0} | all-to-all | bytes 262144 | tf_op jit(solution)/shard_map/all_to_all | solution.py:25
  46.1 0.9 reduce
  47.1 0.2 reshape.22
  47.3 0.2 copy.6
  47.5 0.8 reshape.18
  48.3 0.0 reduce-scatter.2.cloned.1.call-start
  48.3 25.2 %all-gather.5.cloned.1.call-done = f32[512,1024]{1,0:T(8,128)} async-done(((f32[64,1024]{1,0:T(8,128)}), f32[512,1024]{1,0:T(8,128)}) %all-gather.5.cloned.1.call-update) | async-done | bytes 2097168 | tf_op jit(solution)/shard_map/all_gather | solution.py:33
  73.5 68.3 %all-gather.3.cloned.1.call-done = f32[512,1024]{1,0:T(8,128)} async-done(((f32[32,1024]{1,0:T(8,128)}), f32[512,1024]{1,0:T(8,128)}) %all-gather.3.cloned.1.call-update) | async-done | bytes 2097168 | tf_op jit(solution)/shard_map/all_gather | solution.py:27
  141.8 10.2 %fusion = f32[1024,1024]{1,0:T(8,128)} fusion(f32[512,1024]{1,0:T(8,128)} %all-gather.3.cloned.1.call-done, f32[512,1024]{1,0:T(8,128)} %all-gather.5.cloned.1.call-done), kind=kOutput, calls=%fused_computation.3 | convolution fusion | flops 6442450944 | bytes 8388608 | tf_op jit(solution)/shard_map/dot_general | solution.py:10
  152.0 88.2 %reduce-scatter.2.cloned.1.call-done = f32[256,1024]{1,0:T(8,128)} async-done(((f32[1024,1024]{1,0:T(8,128)}), f32[256,1024]{1,0:T(8,128)}) %reduce-scatter.2.cloned.1.call-update) | async-done | bytes 1048592 | tf_op jit(solution)/shard_map/reduce_scatter | solution.py:34
  (6 shorter events, 0.1 us)
Async XLA Ops:
  6.5 66.9 %all-gather.5.cloned.1.call-start = ((), (), s32[]{:S(2)}) async-start(), calls=%async_computation.4 | async-start | bytes 2359296 | tf_op jit(solution)/shard_map/all_gather | solution.py:33
  8.1 19.8 %copy-start = (f32[32,1024]{1,0:T(8,128)S(1)}, f32[32,1024]{1,0:T(8,128)}, u32[]{:S(2)}) copy-start(f32[32,1024]{1,0:T(8,128)} %param.2) | copy-start | bytes 393220
  27.9 113.9 %all-gather.3.cloned.1.call-start = ((), (), s32[]{:S(2)}) async-start(), calls=%async_computation.3 | async-start | bytes 2228224 | tf_op jit(solution)/shard_map/all_gather | solution.py:27
  48.3 191.9 %reduce-scatter.2.cloned.1.call-start = ((), (), s32[]{:S(2)}) async-start(), calls=%async_computation.5 | async-start | bytes 5242880 | tf_op jit(solution)/shard_map/reduce_scatter | solution.py:34
Sparse Core Ops, SparseCore 0:
  28.0 45.4 all-gather.4
  76.8 64.9 all-gather.2
  152.1 88.0 reduce-scatter.1
where the time goes:
time: 247 us
  waiting for transfers between devices  182 us (74%)
  blocking collectives  34.1 us (14%)
  between operations  13.2 us (5%)
  matrix products  10.2 us (4%)
  local copies, waits for them, and re-layouts  5.21 us (2%)
    reduce_scatter x1, waiting for transfers between devices, shards(): lax.psum_scatter(contract(left_band, right_band), 'kpart', scatter_dimens...  88.2 us
    all_gather x1, waiting for transfers between devices, shards(): left_band = lax.all_gather(band_left, 'col', axis=0, tiled=True)  68.3 us
    all_gather x1, waiting for transfers between devices, shards(): right_band = lax.all_gather(band_right, 'row', axis=0, tiled=True)  25.2 us
    all_to_all x1, blocking collectives, shards(): lax.all_to_all(shaped_left, 'row', split_axis=1, concat_axis=3, tiled=True)  17.6 us
    all_to_all x1, blocking collectives, shards(): lax.all_to_all(shaped_right, 'col', split_axis=1, concat_axis=3, tiled=True)  16.5 us
    dot_general x1, matrix products, contract(): lax.dot_general(left_part, right_part, (((0,), (0,)), ((), ())), precisio...  10.2 us
  transfers between devices with their start and end apart: 3, of which 3 were waited for; matrix products, arithmetic and copies ran while one was open for 1% of the time, Pallas kernels for 0%

commit v1 on v0

--- a/solution.py
+++ b/solution.py
@@ -30,7 +30,12 @@
     shaped_right = right_cyclic.reshape(slab_right, column_count, group_right, 1, NB)
     moved_right = lax.all_to_all(shaped_right, "col", split_axis=1, concat_axis=3, tiled=True)
     band_right = moved_right.reshape(slab_right, local_cols)
-    right_band = lax.all_gather(band_right, "row", axis=0, tiled=True)
+    ring = [band_right]
+    for hop in range(7):
+        ring.append(lax.ppermute(ring[-1], "row", [(dev, (dev + 1) % 8) for dev in range(8)]))
+    right_band = jnp.roll(
+        jnp.concatenate(ring[::-1], axis=0), (lax.axis_index("row") + 1) * ring[0].shape[0], axis=0
+    )
     return lax.psum_scatter(
         contract(left_band, right_band), "kpart", scatter_dimension=0, tiled=True
     )

time: 247 us -> 233 us (0.943)
  starting transfers between devices: 0.09 us -> 35.2 us
  blocking collectives: 34.1 us -> 0 us
  waiting for transfers between devices: 182 us -> 150 us
  local copies, waits for them, and re-layouts: 5.21 us -> 20.9 us
    all_gather x1, waiting for transfers between devices: 68.3 us -> 0.01 us  [shards(): left_band = lax.all_gather(band_left, 'col', axis=0, tiled=True)]
    ppermute x0 -> x7, waiting for transfers between devices: none -> 48.9 us  [shards(): lax.ppermute(ring[-1], 'row', [(dev, (dev + 1) % 8) for dev in range(8)])]
    all_to_all x2 -> x0, blocking collectives: 34.1 us -> none  [the longest x1 17.6 us: shards(): lax.all_to_all(shaped_left, 'row', split_axis=1, concat_axis=3, tiled=True)]
    all_gather x1 -> x0, waiting for transfers between devices: 25.2 us -> none  [shards(): right_band = lax.all_gather(band_right, 'row', axis=0, tiled=True)]
    all_to_all x0 -> x2, starting transfers between devices: none -> 21.6 us  [the longest x1 11.6 us: shards(): lax.all_to_all(shaped_right, 'col', split_axis=1, concat_axis=3, tiled=True)]
    ppermute x0 -> x7, starting transfers between devices: none -> 13.5 us  [shards(): lax.ppermute(ring[-1], 'row', [(dev, (dev + 1) % 8) for dev in range(8)])]
    unnamed x6 -> x19, local copies, waits for them, and re-layouts: 1 us -> 13.2 us
    all_to_all x0 -> x2, waiting for transfers between devices: none -> 9.29 us  [the longest x1 5.47 us: shards(): lax.all_to_all(shaped_left, 'row', split_axis=1, concat_axis=3, tiled=True)]
  transfers between devices with their start and end apart: 3 -> 11, of which waited for: 3 -> 10; matrix products, arithmetic and copies ran while one was open for 1% -> 8% of each run, Pallas kernels for 0% -> 0%
where the time goes in v1:
time: 233 us; the launch traced here: 232 us
  waiting for transfers between devices  150 us (64%)
  starting transfers between devices  35.2 us (15%)
  local copies, waits for them, and re-layouts  20.9 us (9%)
  between operations  13.6 us (6%)
  matrix products  10.2 us (4%)
    reduce_scatter x1, waiting for transfers between devices, shards(): lax.psum_scatter(contract(left_band, right_band), 'kpart', scatter_dimens...  92 us
    ppermute x7, waiting for transfers between devices, shards(): lax.ppermute(ring[-1], 'row', [(dev, (dev + 1) % 8) for dev in range(8)])  48.9 us
    ppermute x7, starting transfers between devices, shards(): lax.ppermute(ring[-1], 'row', [(dev, (dev + 1) % 8) for dev in range(8)])  13.5 us
    unnamed x19, local copies, waits for them, and re-layouts  13.2 us
    all_to_all x1, starting transfers between devices, shards(): lax.all_to_all(shaped_right, 'col', split_axis=1, concat_axis=3, tiled=True)  11.6 us
    dot_general x1, matrix products, contract(): lax.dot_general(left_part, right_part, (((0,), (0,)), ((), ())), precisio...  10.2 us
    all_to_all x1, starting transfers between devices, shards(): lax.all_to_all(shaped_left, 'row', split_axis=1, concat_axis=3, tiled=True)  10 us
    all_to_all x1, waiting for transfers between devices, shards(): lax.all_to_all(shaped_left, 'row', split_axis=1, concat_axis=3, tiled=True)  5.47 us
  transfers between devices with their start and end apart: 11, of which 10 were waited for; matrix products, arithmetic and copies ran while one was open for 8% of the time, Pallas kernels for 0%

profile of v1, /device:TPU:57, one launch (start us, length us, event | category | flops | bytes accessed | tf_op | source)
XLA Modules:
  0.0 232.3 jit_solution(6018949823172394747)
XLA Ops:
  6.5 1.1 reshape.19
  8.7 10.0 %all-to-all-start.1 = ((f32[8,1,4096]{2,1,0:T(1,128)}), f32[8,1,4096]{2,1,0:T(1,128)S(1)}, u32[]{:S(2)}, u32[]{:S(2)}) async-start(f32[8,1,4096]{2,1,0:T(1,128)} %reshape.21), calls=%async_computation.1 | async-start | bytes 262144 | tf_op jit(solution)/shard_map/all_to_all | solution.py:25
  18.7 1.1 reshape.17
  21.0 5.5 %all-to-all-done.1 = f32[8,1,4096]{2,1,0:T(1,128)S(1)} async-done(((f32[8,1,4096]{2,1,0:T(1,128)}), f32[8,1,4096]{2,1,0:T(1,128)S(1)}, u32[]{:S(2)}, u32[]{:S(2)}) %all-to-all-start.1) | async-done | bytes 131104 | tf_op jit(solution)/shard_map/all_to_all | solution.py:25
  26.5 11.6 %all-to-all-start = ((f32[16,1,4096]{2,1,0:T(1,128)}), f32[16,1,4096]{2,1,0:T(1,128)S(1)}, u32[]{:S(2)}, u32[]{:S(2)}) async-start(f32[16,1,4096]{2,1,0:T(1,128)} %reshape.23), calls=%async_computation | async-start | bytes 524288 | tf_op jit(solution)/shard_map/all_to_all | solution.py:31
  40.8 3.8 %all-to-all-done = f32[16,1,4096]{2,1,0:T(1,128)S(1)} async-done(((f32[16,1,4096]{2,1,0:T(1,128)}), f32[16,1,4096]{2,1,0:T(1,128)S(1)}, u32[]{:S(2)}, u32[]{:S(2)}) %all-to-all-start) | async-done | bytes 262176 | tf_op jit(solution)/shard_map/all_to_all | solution.py:31
  44.7 1.2 reduce.1
  46.6 2.0 collective-permute-start
  48.6 8.5 %collective-permute-done = f32[64,1024]{1,0:T(8,128)S(1)} collective-permute-done((f32[64,1024]{1,0:T(8,128)S(1)}, f32[64,1024]{1,0:T(8,128)S(1)}, u32[]{:S(2)}, u32[]{:S(2)}) %collective-permute-start) | collective-permute-done | bytes 262176 | tf_op jit(solution)/shard_map/ppermute | solution.py:35
  57.1 1.9 collective-permute-start.1
  59.0 7.7 %collective-permute-done.1 = f32[64,1024]{1,0:T(8,128)S(1)} collective-permute-done((f32[64,1024]{1,0:T(8,128)S(1)}, f32[64,1024]{1,0:T(8,128)S(1)}, u32[]{:S(2)}, u32[]{:S(2)}) %collective-permute-start.1) | collective-permute-done | bytes 262176 | tf_op jit(solution)/shard_map/ppermute | solution.py:35
  66.7 1.9 collective-permute-start.2
  68.6 6.7 %collective-permute-done.2 = f32[64,1024]{1,0:T(8,128)S(1)} collective-permute-done((f32[64,1024]{1,0:T(8,128)S(1)}, f32[64,1024]{1,0:T(8,128)S(1)}, u32[]{:S(2)}, u32[]{:S(2)}) %collective-permute-start.2) | collective-permute-done | bytes 262176 | tf_op jit(solution)/shard_map/ppermute | solution.py:35
  75.3 1.9 collective-permute-start.3
  77.3 6.8 %collective-permute-done.3 = f32[64,1024]{1,0:T(8,128)S(1)} collective-permute-done((f32[64,1024]{1,0:T(8,128)S(1)}, f32[64,1024]{1,0:T(8,128)S(1)}, u32[]{:S(2)}, u32[]{:S(2)}) %collective-permute-start.3) | collective-permute-done | bytes 262176 | tf_op jit(solution)/shard_map/ppermute | solution.py:35
  84.1 1.9 collective-permute-start.4
  86.0 6.4 %collective-permute-done.4 = f32[64,1024]{1,0:T(8,128)S(1)} collective-permute-done((f32[64,1024]{1,0:T(8,128)S(1)}, f32[64,1024]{1,0:T(8,128)S(1)}, u32[]{:S(2)}, u32[]{:S(2)}) %collective-permute-start.4) | collective-permute-done | bytes 262176 | tf_op jit(solution)/shard_map/ppermute | solution.py:35
  92.4 1.9 collective-permute-start.5
  94.3 6.4 %collective-permute-done.5 = f32[64,1024]{1,0:T(8,128)S(1)} collective-permute-done((f32[64,1024]{1,0:T(8,128)S(1)}, f32[64,1024]{1,0:T(8,128)S(1)}, u32[]{:S(2)}, u32[]{:S(2)}) %collective-permute-start.5) | collective-permute-done | bytes 262176 | tf_op jit(solution)/shard_map/ppermute | solution.py:35
  100.7 1.9 collective-permute-start.6
  102.6 6.4 %collective-permute-done.6 = f32[64,1024]{1,0:T(8,128)S(1)} collective-permute-done((f32[64,1024]{1,0:T(8,128)S(1)}, f32[64,1024]{1,0:T(8,128)S(1)}, u32[]{:S(2)}, u32[]{:S(2)}) %collective-permute-start.6) | collective-permute-done | bytes 262176 | tf_op jit(solution)/shard_map/ppermute | solution.py:35
  120.7 10.2 %convolution_bitcast_fusion = f32[1024,1024]{0,1:T(8,128)} fusion(f32[512,1024]{1,0:T(8,128)} %all-gather.2.cloned.1.call-done, f32[1024,1024]{1,0:T(8,128)} %constant_dynamic-update-slice_fusion, s32[]{:T(128)S(6)} %select_n.14), kind=kOutput, calls=%fused_computation | convolution fusion | flops 6442450944 | bytes 8388612 | tf_op jit(solution)/shard_map/dot_general | solution.py:10
  130.9 92.0 %reduce-scatter.2.cloned.1.call-done = f32[256,1024]{0,1:T(8,128)} async-done(((f32[1024,1024]{0,1:T(8,128)}), f32[256,1024]{0,1:T(8,128)}) %reduce-scatter.2.cloned.1.call-update) | async-done | bytes 1048592 | tf_op jit(solution)/shard_map/reduce_scatter | solution.py:39
  222.9 2.5 %copy.12 = f32[256,1024]{1,0:T(8,128)} copy(f32[256,1024]{0,1:T(8,128)} %reduce-scatter.2.cloned.1.call-done) | data formatting | bytes 2097152 | tf_op jit(solution)/shard_map/reduce_scatter | solution.py:39
  (34 shorter events, 17.3 us)
Async XLA Ops:
  8.7 17.8 %all-to-all-start.1 = ((f32[8,1,4096]{2,1,0:T(1,128)}), f32[8,1,4096]{2,1,0:T(1,128)S(1)}, u32[]{:S(2)}, u32[]{:S(2)}) async-start(f32[8,1,4096]{2,1,0:T(1,128)} %reshape.21), calls=%async_computation.1 | async-start | bytes 262144 | tf_op jit(solution)/shard_map/all_to_all | solution.py:25
  26.5 18.2 %all-to-all-start = ((f32[16,1,4096]{2,1,0:T(1,128)}), f32[16,1,4096]{2,1,0:T(1,128)S(1)}, u32[]{:S(2)}, u32[]{:S(2)}) async-start(f32[16,1,4096]{2,1,0:T(1,128)} %reshape.23), calls=%async_computation | async-start | bytes 524288 | tf_op jit(solution)/shard_map/all_to_all | solution.py:31
  38.1 82.6 %all-gather.2.cloned.1.call-start = ((), (), s32[]{:S(2)}) async-start(), calls=%async_computation.3 | async-start | bytes 2228224 | tf_op jit(solution)/shard_map/all_gather | solution.py:27
  40.8 182.1 %reduce-scatter.2.cloned.1.call-start = ((), (), s32[]{:S(2)}) async-start(), calls=%async_computation.4 | async-start | bytes 5242880 | tf_op jit(solution)/shard_map/reduce_scatter | solution.py:39
  46.6 10.5 %collective-permute-start = (f32[64,1024]{1,0:T(8,128)S(1)}, f32[64,1024]{1,0:T(8,128)S(1)}, u32[]{:S(2)}, u32[]{:S(2)}) collective-permute-start(f32[64,1024]{1,0:T(8,128)S(1)} %reshape.18), channel_id=1, source_target_pairs={{0,64},{64,128},{128,192},{192,256},{256,320},{320,384},{384,448},... | collective-permute-start | bytes 786440 | tf_op jit(solution)/shard_map/ppermute | solution.py:35
  57.1 9.6 %collective-permute-start.1 = (f32[64,1024]{1,0:T(8,128)S(1)}, f32[64,1024]{1,0:T(8,128)S(1)}, u32[]{:S(2)}, u32[]{:S(2)}) collective-permute-start(f32[64,1024]{1,0:T(8,128)S(1)} %collective-permute-done), channel_id=1, source_target_pairs={{0,64},{64,128},{128,192},{192,256},{256,320},{320,384},{384,448},... | collective-permute-start | bytes 786440 | tf_op jit(solution)/shard_map/ppermute | solution.py:35
  66.7 8.6 %collective-permute-start.2 = (f32[64,1024]{1,0:T(8,128)S(1)}, f32[64,1024]{1,0:T(8,128)S(1)}, u32[]{:S(2)}, u32[]{:S(2)}) collective-permute-start(f32[64,1024]{1,0:T(8,128)S(1)} %collective-permute-done.1), channel_id=1, source_target_pairs={{0,64},{64,128},{128,192},{192,256},{256,320},{320,384},{384,448},... | collective-permute-start | bytes 786440 | tf_op jit(solution)/shard_map/ppermute | solution.py:35
  75.3 8.7 %collective-permute-start.3 = (f32[64,1024]{1,0:T(8,128)S(1)}, f32[64,1024]{1,0:T(8,128)S(1)}, u32[]{:S(2)}, u32[]{:S(2)}) collective-permute-start(f32[64,1024]{1,0:T(8,128)S(1)} %collective-permute-done.2), channel_id=1, source_target_pairs={{0,64},{64,128},{128,192},{192,256},{256,320},{320,384},{384,448},... | collective-permute-start | bytes 786440 | tf_op jit(solution)/shard_map/ppermute | solution.py:35
  84.1 8.3 %collective-permute-start.4 = (f32[64,1024]{1,0:T(8,128)S(1)}, f32[64,1024]{1,0:T(8,128)S(1)}, u32[]{:S(2)}, u32[]{:S(2)}) collective-permute-start(f32[64,1024]{1,0:T(8,128)S(1)} %collective-permute-done.3), channel_id=1, source_target_pairs={{0,64},{64,128},{128,192},{192,256},{256,320},{320,384},{384,448},... | collective-permute-start | bytes 786440 | tf_op jit(solution)/shard_map/ppermute | solution.py:35
  92.4 8.3 %collective-permute-start.5 = (f32[64,1024]{1,0:T(8,128)S(1)}, f32[64,1024]{1,0:T(8,128)S(1)}, u32[]{:S(2)}, u32[]{:S(2)}) collective-permute-start(f32[64,1024]{1,0:T(8,128)S(1)} %collective-permute-done.4), channel_id=1, source_target_pairs={{0,64},{64,128},{128,192},{192,256},{256,320},{320,384},{384,448},... | collective-permute-start | bytes 786440 | tf_op jit(solution)/shard_map/ppermute | solution.py:35
  100.7 8.3 %collective-permute-start.6 = (f32[64,1024]{1,0:T(8,128)S(1)}, f32[64,1024]{1,0:T(8,128)S(1)}, u32[]{:S(2)}, u32[]{:S(2)}) collective-permute-start(f32[64,1024]{1,0:T(8,128)S(1)} %collective-permute-done.5), channel_id=1, source_target_pairs={{0,64},{64,128},{128,192},{192,256},{256,320},{320,384},{384,448},... | collective-permute-start | bytes 786440 | tf_op jit(solution)/shard_map/ppermute | solution.py:35
Sparse Core Ops, SparseCore 0:
  42.2 57.9 all-gather.1
  131.0 91.8 reduce-scatter.1
